TPU v7x, 512 devices: a whole 4x4x16 slice. The times are simulated.
512 devices in a mesh: facet: 16 (over x_lo, y, core), pulse: 32 (over x_hi, z).
Axes of the slice: x: 4 (x_hi: 2, x_lo: 2; x = x_hi * 2 + x_lo), y: 4, z: 16, core: 2. Of those that a mesh axis runs over, the one named last changes fastest.
Arguments:
- facet_positions: float32 [3, 12288], P(None, 'facet'), may hold values from -10 to 10
- reflectivity: float32 [2, 12288], P(None, 'facet'), may hold values from -0.078125 to 0.078125
- block_building: int32 [96], P('facet'), may hold values from 0 to 23, never falling along the last dimension, each value on 1 to 8 neighbouring positions
- visible: int32 [24, 64], P(None, 'pulse'), may hold values from 0 to 1
- platform: float32 [3, 2048], P(None, 'pulse'), may hold values from 30 to 40
Outputs:
- image: float32 [2, 512, 2048], P(None, 'pulse', 'facet')
All inputs are finite; a program needn't handle non-finite values.
Results may differ from a plain program's by a relative error of at most 0.017.
Values may be sent and summed in bfloat16 or wider, within the bound.
A program may use at most 64 MiB of HBM per device.

v0:
```python
import math

import jax
import jax.numpy as jnp
from jax import lax
from jax.sharding import Mesh
from jax.sharding import PartitionSpec as P

F_DEV = 768
BLK = 128
PULSES = 2048
PBS = 32
BINS = 512
BIN_LO = 32
BIN_HI = 16
PULSE = ("pulse_0", "pulse_1")


wave_start = 2.0
wave_step = 0.25


def from_everyone(shard, axis):
    copies = jnp.broadcast_to(shard, (lax.axis_size(axis), *shard.shape))
    return lax.all_to_all(copies, axis, split_axis=0, concat_axis=0, tiled=True)


def in_order(pieces, dim):
    pieces = jnp.moveaxis(pieces, 0, dim)
    dims = pieces.shape
    return pieces.reshape(*dims[:dim], dims[dim] * dims[dim + 1], *dims[dim + 2 :])


def gathered_copies(shard, axis, dim):
    pieces = from_everyone(shard, axis)
    return in_order(pieces, dim)


def in_blocks(shard, dim, count):
    before, after = (shard.shape[:dim], shard.shape[dim + 1 :])
    return jnp.moveaxis(shard.reshape(*before, count, -1, *after), dim, 0)


def exchange_in_order(pieces, axes, sequence):
    dims = [lax.axis_size(a) for a in axes]
    pieces = pieces.reshape(*dims, *pieces.shape[1:])
    for k in sequence:
        pieces = lax.all_to_all(pieces, axes[k], split_axis=k, concat_axis=k, tiled=True)
    return pieces.reshape(-1, *pieces.shape[len(axes) :])


def one_axis_at_a_time(shard, axes, sequence, split_dim, concat_dim):
    pieces = in_blocks(shard, split_dim, lax.axis_size(axes))
    return in_order(exchange_in_order(pieces, axes, sequence), concat_dim)


def echo_group(positions, weights, antenna):
    offsets = positions[:, None, :] - antenna[:, :, None]
    distance = jnp.sqrt(jnp.sum(offsets * offsets, axis=0))
    upper_index = jnp.arange(BIN_HI, dtype=jnp.float32)
    lower_index = jnp.arange(BIN_LO, dtype=jnp.float32)
    coarse = (wave_start + wave_step * BIN_LO * upper_index)[None, :, None] * distance[:, None, :]
    cosine = jnp.cos(coarse)
    sine_a = jnp.sin(coarse)
    real_a = weights[0][None, None, :] * cosine + weights[1][None, None, :] * sine_a
    imag_a = weights[1][None, None, :] * cosine - weights[0][None, None, :] * sine_a
    table_a = jnp.concatenate([real_a, imag_a], axis=1).astype(jnp.bfloat16)
    phase_b = (wave_step * lower_index)[None, :, None] * distance[:, None, :]
    table_b = jnp.concatenate([jnp.cos(phase_b), -jnp.sin(phase_b)], axis=1).astype(jnp.bfloat16)
    products = jnp.einsum("gan,gbn->gab", table_a, table_b, preferred_element_type=jnp.float32)
    real_part = products[:, :BIN_HI, :BIN_LO] - products[:, BIN_HI:, BIN_LO:]
    imag_part = products[:, :BIN_HI, BIN_LO:] + products[:, BIN_HI:, :BIN_LO]
    return jnp.stack([real_part, imag_part]).reshape(2, antenna.shape[1], BINS)


def echo_pulses(packed, antenna, pulse_first):
    pulse_total = antenna.shape[1]
    group_len = min(8, pulse_total)

    def group_step(state_unused, group_index):
        first_pulse = group_index * group_len
        block_index = (pulse_first + first_pulse) // PBS
        weights = lax.dynamic_slice_in_dim(packed, 3 + 2 * block_index, 2, 0)
        return (state_unused, echo_group(packed[:3], weights, antenna))

    unused_state, groups = lax.scan(
        group_step, jnp.int32(0), jnp.arange(pulse_total // group_len, dtype=jnp.int32)
    )
    return groups.transpose(1, 3, 0, 2).reshape(2, BINS, pulse_total)


def echo_tiles(packed, antenna, pulse_first):
    tile_count = packed.shape[1] // F_DEV

    def tile_step(tile_index, running):
        tile_rows = lax.dynamic_slice_in_dim(packed, tile_index * F_DEV, F_DEV, 1)
        return running + echo_pulses(tile_rows, antenna, pulse_first)

    return lax.fori_loop(
        0, tile_count, tile_step, jnp.zeros((2, BINS, antenna.shape[1]), jnp.float32)
    )


def contract(left_side, right_side):
    return lax.dot_general(
        left_side, right_side, (((1,), (1,)), ((), ())), preferred_element_type=jnp.float32
    )


def spectrum_part(echoes, pulse_ids, k_rows):
    angle_grid = (
        2.0 * math.pi / PULSES * (k_rows[:, None] * pulse_ids[None, :] % PULSES).astype(jnp.float32)
    )
    scale_w = 1.0 / math.sqrt(PULSES)
    w_real = (jnp.cos(angle_grid) * scale_w).astype(jnp.bfloat16)
    w_imag = (-jnp.sin(angle_grid) * scale_w).astype(jnp.bfloat16)
    real_s = contract(echoes[0], w_real) - contract(echoes[1], w_imag)
    imag_s = contract(echoes[0], w_imag) + contract(echoes[1], w_real)
    return jnp.stack([real_s, imag_s])


def chirp_apply(spectrum, bin_rows, k_rows):
    offset_k = (k_rows - PULSES // 2).astype(jnp.float32)
    wave_bin = wave_start + wave_step * bin_rows.astype(jnp.float32)
    phase = jnp.pi * (offset_k * offset_k / PULSES)[None, :] * (wave_start / wave_bin)[:, None]
    cosine = jnp.cos(phase)
    sine_h = jnp.sin(phase)
    return jnp.stack(
        [cosine * spectrum[0] - sine_h * spectrum[1], cosine * spectrum[1] + sine_h * spectrum[0]]
    )


def body(facet_positions, reflectivity, block_building, visible, platform):
    facet_count = lax.axis_size("facet")
    pulse_count = lax.axis_size(PULSE)
    facets_here = facet_positions.shape[1]
    pulse_dev = platform.shape[1]
    bins_dev = BINS // pulse_count
    k_block = PULSES // facet_count
    k_rows = lax.axis_index("facet") * k_block + jnp.arange(k_block, dtype=jnp.int32)
    bin_rows = lax.axis_index(PULSE) * bins_dev + jnp.arange(bins_dev, dtype=jnp.int32)
    seen_blocks = jnp.take(visible, block_building, axis=0).astype(jnp.float32)
    seen_facets = jnp.repeat(seen_blocks.T, BLK, axis=1)
    weighted = (reflectivity[None, :, :] * seen_facets[:, None, :]).reshape(-1, facets_here)
    packed = jnp.concatenate([facet_positions, weighted], axis=0)
    share = pulse_dev // facet_count
    first_mine = lax.axis_index("facet") * share
    antenna = lax.dynamic_slice_in_dim(platform, first_mine, share, 1)
    total = echo_tiles(gathered_copies(packed, "facet", 1), antenna, first_mine)
    turned = one_axis_at_a_time(total.astype(jnp.bfloat16), PULSE, (0, 1), 1, 2)
    echo_piece = gathered_copies(turned, "facet", 2)
    places = jnp.arange(echo_piece.shape[2], dtype=jnp.int32)
    outer_index = places // (pulse_count * share)
    middle_index = places // share % pulse_count
    inner_index = places % share
    pulse_ids = middle_index * pulse_dev + outer_index * share + inner_index
    spectrum = spectrum_part(echo_piece, pulse_ids, k_rows)
    return chirp_apply(spectrum, bin_rows, k_rows)


def solution(mesh):
    torus = Mesh(mesh.devices.reshape(mesh.shape["facet"], 2, 16), ("facet", "pulse_0", "pulse_1"))
    placed = (P(None, "facet"), P(None, "facet"), P("facet"), P(None, PULSE), P(None, PULSE))
    return jax.shard_map(
        body, mesh=torus, in_specs=placed, out_specs=P(None, PULSE, "facet"), check_vma=False
    )
```

profile of v0, /device:TPU:1, one launch (start us, length us, event | category | flops | bytes accessed | tf_op | source)
XLA Modules:
  0.0 138.4 jit_solution(3638425582657081141)
XLA Ops:
  4.5 10.2 %all-to-all-start = ((f32[16,7,768]{2,1,0:T(8,128)}), f32[16,7,768]{2,1,0:T(8,128)S(1)}, u32[]{:S(2)}, u32[]{:S(2)}) async-start(f32[16,7,768]{2,1,0:T(8,128)} %broadcast_in_dim.55), calls=%async_computation | async-start | bytes 786432 | tf_op jit(solution)/shard_map/all_to_all | solution.py:25
  14.8 8.4 %all-to-all-done = f32[16,7,768]{2,1,0:T(8,128)S(1)} async-done(((f32[16,7,768]{2,1,0:T(8,128)}), f32[16,7,768]{2,1,0:T(8,128)S(1)}, u32[]{:S(2)}, u32[]{:S(2)}) %all-to-all-start) | async-done | bytes 344096 | tf_op jit(solution)/shard_map/all_to_all | solution.py:25
  23.2 51.0 %while.25 = (s32[]{:T(128)}, f32[2,512,4]{1,2,0:T(4,128)S(1)}, f32[7,12288]{1,0:T(8,128)S(1)}, s32[]{:T(128)}, f32[3,4]{1,0:T(4,128)S(1)}, /*index=5*/s32[]{:T(1...) while((s32[]{:T(128)}, f32[2,512,4]{1,2,0:T(4,128)S(1)}, ...), condition=%wide.region_2.3_spmd.clone, body=%wide.region_0.0_spmd.clone.sunk | while | flops 14639177 | bytes 1451649 | solution.py:99
  23.4 0.8 fusion.87
  24.2 1.6 %fusion.86 = (bf16[4,32,768]{2,1,0:T(8,128)(2,1)S(1)}, bf16[4,32,768]{2,1,0:T(8,128)(2,1)S(1)}) fusion(f32[4,768]{1,0:T(4,128)S(1)} %sqrt.18, f32[32]{0:T(128)S(1)} %iota_multiply_fusion.2), kind=kLoop, calls=%fused_computation.3.clone.1 | loop fusion | flops 393216 | bytes 405632 | tf_op jit(solution)/shard_map/convert
  26.6 0.8 fusion.87
  27.4 1.6 %fusion.86 = (bf16[4,32,768]{2,1,0:T(8,128)(2,1)S(1)}, bf16[4,32,768]{2,1,0:T(8,128)(2,1)S(1)}) fusion(f32[4,768]{1,0:T(4,128)S(1)} %sqrt.18, f32[32]{0:T(128)S(1)} %iota_multiply_fusion.2), kind=kLoop, calls=%fused_computation.3.clone.1 | loop fusion | flops 393216 | bytes 405632 | tf_op jit(solution)/shard_map/convert
  30.6 1.6 %fusion.86 = (bf16[4,32,768]{2,1,0:T(8,128)(2,1)S(1)}, bf16[4,32,768]{2,1,0:T(8,128)(2,1)S(1)}) fusion(f32[4,768]{1,0:T(4,128)S(1)} %sqrt.18, f32[32]{0:T(128)S(1)} %iota_multiply_fusion.2), kind=kLoop, calls=%fused_computation.3.clone.1 | loop fusion | flops 393216 | bytes 405632 | tf_op jit(solution)/shard_map/convert
  33.0 0.8 fusion.87
  33.8 1.6 %fusion.86 = (bf16[4,32,768]{2,1,0:T(8,128)(2,1)S(1)}, bf16[4,32,768]{2,1,0:T(8,128)(2,1)S(1)}) fusion(f32[4,768]{1,0:T(4,128)S(1)} %sqrt.18, f32[32]{0:T(128)S(1)} %iota_multiply_fusion.2), kind=kLoop, calls=%fused_computation.3.clone.1 | loop fusion | flops 393216 | bytes 405632 | tf_op jit(solution)/shard_map/convert
  37.0 1.6 %fusion.86 = (bf16[4,32,768]{2,1,0:T(8,128)(2,1)S(1)}, bf16[4,32,768]{2,1,0:T(8,128)(2,1)S(1)}) fusion(f32[4,768]{1,0:T(4,128)S(1)} %sqrt.18, f32[32]{0:T(128)S(1)} %iota_multiply_fusion.2), kind=kLoop, calls=%fused_computation.3.clone.1 | loop fusion | flops 393216 | bytes 405632 | tf_op jit(solution)/shard_map/convert
  40.2 1.6 %fusion.86 = (bf16[4,32,768]{2,1,0:T(8,128)(2,1)S(1)}, bf16[4,32,768]{2,1,0:T(8,128)(2,1)S(1)}) fusion(f32[4,768]{1,0:T(4,128)S(1)} %sqrt.18, f32[32]{0:T(128)S(1)} %iota_multiply_fusion.2), kind=kLoop, calls=%fused_computation.3.clone.1 | loop fusion | flops 393216 | bytes 405632 | tf_op jit(solution)/shard_map/convert
  43.4 1.6 %fusion.86 = (bf16[4,32,768]{2,1,0:T(8,128)(2,1)S(1)}, bf16[4,32,768]{2,1,0:T(8,128)(2,1)S(1)}) fusion(f32[4,768]{1,0:T(4,128)S(1)} %sqrt.18, f32[32]{0:T(128)S(1)} %iota_multiply_fusion.2), kind=kLoop, calls=%fused_computation.3.clone.1 | loop fusion | flops 393216 | bytes 405632 | tf_op jit(solution)/shard_map/convert
  46.6 1.6 %fusion.86 = (bf16[4,32,768]{2,1,0:T(8,128)(2,1)S(1)}, bf16[4,32,768]{2,1,0:T(8,128)(2,1)S(1)}) fusion(f32[4,768]{1,0:T(4,128)S(1)} %sqrt.18, f32[32]{0:T(128)S(1)} %iota_multiply_fusion.2), kind=kLoop, calls=%fused_computation.3.clone.1 | loop fusion | flops 393216 | bytes 405632 | tf_op jit(solution)/shard_map/convert
  49.8 1.6 %fusion.86 = (bf16[4,32,768]{2,1,0:T(8,128)(2,1)S(1)}, bf16[4,32,768]{2,1,0:T(8,128)(2,1)S(1)}) fusion(f32[4,768]{1,0:T(4,128)S(1)} %sqrt.18, f32[32]{0:T(128)S(1)} %iota_multiply_fusion.2), kind=kLoop, calls=%fused_computation.3.clone.1 | loop fusion | flops 393216 | bytes 405632 | tf_op jit(solution)/shard_map/convert
  53.0 1.6 %fusion.86 = (bf16[4,32,768]{2,1,0:T(8,128)(2,1)S(1)}, bf16[4,32,768]{2,1,0:T(8,128)(2,1)S(1)}) fusion(f32[4,768]{1,0:T(4,128)S(1)} %sqrt.18, f32[32]{0:T(128)S(1)} %iota_multiply_fusion.2), kind=kLoop, calls=%fused_computation.3.clone.1 | loop fusion | flops 393216 | bytes 405632 | tf_op jit(solution)/shard_map/convert
  56.1 1.6 %fusion.86 = (bf16[4,32,768]{2,1,0:T(8,128)(2,1)S(1)}, bf16[4,32,768]{2,1,0:T(8,128)(2,1)S(1)}) fusion(f32[4,768]{1,0:T(4,128)S(1)} %sqrt.18, f32[32]{0:T(128)S(1)} %iota_multiply_fusion.2), kind=kLoop, calls=%fused_computation.3.clone.1 | loop fusion | flops 393216 | bytes 405632 | tf_op jit(solution)/shard_map/convert
  59.3 1.6 %fusion.86 = (bf16[4,32,768]{2,1,0:T(8,128)(2,1)S(1)}, bf16[4,32,768]{2,1,0:T(8,128)(2,1)S(1)}) fusion(f32[4,768]{1,0:T(4,128)S(1)} %sqrt.18, f32[32]{0:T(128)S(1)} %iota_multiply_fusion.2), kind=kLoop, calls=%fused_computation.3.clone.1 | loop fusion | flops 393216 | bytes 405632 | tf_op jit(solution)/shard_map/convert
  62.5 1.6 %fusion.86 = (bf16[4,32,768]{2,1,0:T(8,128)(2,1)S(1)}, bf16[4,32,768]{2,1,0:T(8,128)(2,1)S(1)}) fusion(f32[4,768]{1,0:T(4,128)S(1)} %sqrt.18, f32[32]{0:T(128)S(1)} %iota_multiply_fusion.2), kind=kLoop, calls=%fused_computation.3.clone.1 | loop fusion | flops 393216 | bytes 405632 | tf_op jit(solution)/shard_map/convert
  65.7 1.6 %fusion.86 = (bf16[4,32,768]{2,1,0:T(8,128)(2,1)S(1)}, bf16[4,32,768]{2,1,0:T(8,128)(2,1)S(1)}) fusion(f32[4,768]{1,0:T(4,128)S(1)} %sqrt.18, f32[32]{0:T(128)S(1)} %iota_multiply_fusion.2), kind=kLoop, calls=%fused_computation.3.clone.1 | loop fusion | flops 393216 | bytes 405632 | tf_op jit(solution)/shard_map/convert
  68.9 1.6 %fusion.86 = (bf16[4,32,768]{2,1,0:T(8,128)(2,1)S(1)}, bf16[4,32,768]{2,1,0:T(8,128)(2,1)S(1)}) fusion(f32[4,768]{1,0:T(4,128)S(1)} %sqrt.18, f32[32]{0:T(128)S(1)} %iota_multiply_fusion.2), kind=kLoop, calls=%fused_computation.3.clone.1 | loop fusion | flops 393216 | bytes 405632 | tf_op jit(solution)/shard_map/convert
  72.1 1.6 %fusion.86 = (bf16[4,32,768]{2,1,0:T(8,128)(2,1)S(1)}, bf16[4,32,768]{2,1,0:T(8,128)(2,1)S(1)}) fusion(f32[4,768]{1,0:T(4,128)S(1)} %sqrt.18, f32[32]{0:T(128)S(1)} %iota_multiply_fusion.2), kind=kLoop, calls=%fused_computation.3.clone.1 | loop fusion | flops 393216 | bytes 405632 | tf_op jit(solution)/shard_map/convert
  75.1 3.2 %all-to-all-start.1 = ((bf16[2,2,1024]{2,1,0:T(2,128)(2,1)}), bf16[2,2,1024]{2,1,0:T(2,128)(2,1)S(1)}, u32[]{:S(2)}, u32[]{:S(2)}) async-start(bf16[2,2,1024]{2,1,0:T(2,128)(2,1)} %reshape.163), calls=%async_computation.1 | async-start | bytes 16384 | tf_op jit(solution)/shard_map/all_to_all | solution.py:48
  78.3 4.1 %all-to-all-done.1 = bf16[2,2,1024]{2,1,0:T(2,128)(2,1)S(1)} async-done(((bf16[2,2,1024]{2,1,0:T(2,128)(2,1)}), bf16[2,2,1024]{2,1,0:T(2,128)(2,1)S(1)}, u32[]{:S(2)}, u32[]{:S(2)}) %all-to-all-start.1) | async-done | bytes 8224 | tf_op jit(solution)/shard_map/all_to_all | solution.py:48
  83.3 12.0 %all-to-all-start.2 = ((bf16[16,2,128]{2,1,0:T(2,128)(2,1)}), bf16[16,2,128]{2,1,0:T(2,128)(2,1)S(1)}, u32[]{:S(2)}, u32[]{:S(2)}) async-start(bf16[16,2,128]{2,1,0:T(2,128)(2,1)} %reshape.165), calls=%async_computation.2 | async-start | bytes 16384 | tf_op jit(solution)/shard_map/all_to_all | solution.py:48
  95.4 11.2 %all-to-all-done.2 = bf16[16,2,128]{2,1,0:T(2,128)(2,1)S(1)} async-done(((bf16[16,2,128]{2,1,0:T(2,128)(2,1)}), bf16[16,2,128]{2,1,0:T(2,128)(2,1)S(1)}, u32[]{:S(2)}, u32[]{:S(2)}) %all-to-all-start.2) | async-done | bytes 8224 | tf_op jit(solution)/shard_map/all_to_all | solution.py:48
  107.8 7.3 %all-to-all-start.3 = ((bf16[16,2,16,128]{3,2,1,0:T(8,128)(2,1)}), bf16[16,2,16,128]{3,2,1,0:T(8,128)(2,1)S(1)}, u32[]{:S(2)}, u32[]{:S(2)}) async-start(bf16[16,2,16,128]{3,2,1,0:T(8,128)(2,1)} %broadcast_in_dim.56), calls=%async_computation.3 | async-start | bytes 262144 | tf_op jit(solution)/shard_map/all_to_all | solution.py:25
  115.1 6.2 %all-to-all-done.3 = bf16[16,2,16,128]{3,2,1,0:T(8,128)(2,1)S(1)} async-done(((bf16[16,2,16,128]{3,2,1,0:T(8,128)(2,1)}), bf16[16,2,16,128]{3,2,1,0:T(8,128)(2,1)S(1)}, u32[]{:S(2)}, u32[]{:S(2)}) %all-to-all-start.3) | async-done | bytes 131104 | tf_op jit(solution)/shard_map/all_to_all | solution.py:25
  121.4 4.0 %fusion.24 = f32[16,128]{1,0:T(8,128)S(1)} fusion(s32[2048]{0:T(1024)S(1)} %fusion.50, s32[128]{0:T(128)S(1)} %iota_add_fusion, bf16[2,8,16,128]{3,2,1,0:T(8,128)(2,1)S(1)} %bitcast.67), kind=kOutput, calls=%fused_computation.47 | convolution fusion | flops 12845056 | bytes 82432 | tf_op jit(solution)/shard_map/dot_general | solution.py:105
  125.4 4.0 %fusion.23 = f32[16,128]{1,0:T(8,128)S(1)} fusion(s32[2048]{0:T(1024)S(1)} %fusion.50, s32[128]{0:T(128)S(1)} %iota_add_fusion, bf16[2,8,16,128]{3,2,1,0:T(8,128)(2,1)S(1)} %bitcast.68), kind=kOutput, calls=%fused_computation.46 | convolution fusion | flops 12582912 | bytes 82432 | tf_op jit(solution)/shard_map/dot_general | solution.py:105
  129.5 4.2 %convolution_add_fusion = f32[16,128]{1,0:T(8,128)S(1)} fusion(f32[16,128]{1,0:T(8,128)S(1)} %fusion.24, s32[2048]{0:T(1024)S(1)} %fusion.50, s32[128]{0:T(128)S(1)} %iota_add_fusion, bf16[2,8,16,128]{3,2,1,0:T(8,128)(2,1)S(1)} %bitcast.65), kind=kOutput, calls=%fused_computation.39 | convolution fusion | flops 12584960 | bytes 90624 | tf_op jit(solution)/shard_map/dot_general | solution.py:105
  133.7 4.0 %fusion.44 = (f32[1,16,128]{2,1,0:T(8,128)S(1)}, f32[1,16,128]{2,1,0:T(8,128)S(1)}) fusion(f32[16,128]{1,0:T(8,128)S(1)} %convolution_add_fusion, f32[16]{0:T(128)S(1)} %add_divide_fusion, f32[128]{0:T(128)S(1)} %multiply_multiply_fusion, f32[16,128]{1,0:T(8,128)S(1)} %fusion.23, s32[2048]{0:T(1024)S(1)} %fusion.50, s32[128]{0:T(128)S(1)} %iota_add_fusion, ...), kind=kOutput, calls=%fused_computation.81 | convolution fusion | flops 12861440 | bytes 107584 | tf_op jit(solution)/shard_map/dot_general | solution.py:105
  (235 shorter events, 30.2 us)
Async XLA Ops:
  0.0 14.7 %copy-start = (f32[3,64]{1,0:T(4,128)S(1)}, f32[3,64]{1,0:T(4,128)}, u32[]{:S(2)}) copy-start(f32[3,64]{1,0:T(4,128)} %param.11) | copy-start | bytes 2308
  0.0 0.7 copy-start.4
  0.7 0.7 copy-start.3
  2.3 0.7 copy-start.2
  3.0 0.7 copy-start.1
  4.5 18.7 %all-to-all-start = ((f32[16,7,768]{2,1,0:T(8,128)}), f32[16,7,768]{2,1,0:T(8,128)S(1)}, u32[]{:S(2)}, u32[]{:S(2)}) async-start(f32[16,7,768]{2,1,0:T(8,128)} %broadcast_in_dim.55), calls=%async_computation | async-start | bytes 786432 | tf_op jit(solution)/shard_map/all_to_all | solution.py:25
  75.1 7.4 %all-to-all-start.1 = ((bf16[2,2,1024]{2,1,0:T(2,128)(2,1)}), bf16[2,2,1024]{2,1,0:T(2,128)(2,1)S(1)}, u32[]{:S(2)}, u32[]{:S(2)}) async-start(bf16[2,2,1024]{2,1,0:T(2,128)(2,1)} %reshape.163), calls=%async_computation.1 | async-start | bytes 16384 | tf_op jit(solution)/shard_map/all_to_all | solution.py:48
  83.3 23.3 %all-to-all-start.2 = ((bf16[16,2,128]{2,1,0:T(2,128)(2,1)}), bf16[16,2,128]{2,1,0:T(2,128)(2,1)S(1)}, u32[]{:S(2)}, u32[]{:S(2)}) async-start(bf16[16,2,128]{2,1,0:T(2,128)(2,1)} %reshape.165), calls=%async_computation.2 | async-start | bytes 16384 | tf_op jit(solution)/shard_map/all_to_all | solution.py:48
  107.8 13.6 %all-to-all-start.3 = ((bf16[16,2,16,128]{3,2,1,0:T(8,128)(2,1)}), bf16[16,2,16,128]{3,2,1,0:T(8,128)(2,1)S(1)}, u32[]{:S(2)}, u32[]{:S(2)}) async-start(bf16[16,2,16,128]{3,2,1,0:T(8,128)(2,1)} %broadcast_in_dim.56), calls=%async_computation.3 | async-start | bytes 262144 | tf_op jit(solution)/shard_map/all_to_all | solution.py:25
where the time goes:
time: 139 us; the launch traced here: 138 us
  other arithmetic  43.1 us (31%)
  starting transfers between devices  32.8 us (24%)
  waiting for transfers between devices  29.9 us (22%)
  matrix products  19.8 us (14%)
  local copies, waits for them, and re-layouts  11.3 us (8%)
    another operation x32, other arithmetic  38.1 us
    all_to_all x2, starting transfers between devices, from_everyone(): return lax.all_to_all(copies, axis, split_axis=0, concat_axis=0, tiled=True)  17.5 us
    dot_general x4, matrix products, contract(): lax.dot_general(left_side, right_side, (((1,), (1,)), ((), ())), preferre...  16.3 us
    all_to_all x2, waiting for transfers between devices, exchange_in_order(): lax.all_to_all(pieces, axes[k], split_axis=k, concat_axis=k, tiled=True)  15.3 us
    all_to_all x2, starting transfers between devices, exchange_in_order(): lax.all_to_all(pieces, axes[k], split_axis=k, concat_axis=k, tiled=True)  15.3 us
    all_to_all x2, waiting for transfers between devices, from_everyone(): return lax.all_to_all(copies, axis, split_axis=0, concat_axis=0, tiled=True)  14.6 us
    unnamed x17, local copies, waits for them, and re-layouts  3.83 us
    dot_general x16, matrix products, echo_group(): jnp.einsum('gan,gbn->gab', table_a, table_b, preferred_element_type=jnp.f...  3.5 us
  transfers between devices with their start and end apart: 4, of which 4 were waited for; matrix products, arithmetic and copies ran while one was open for 0% of the time, Pallas kernels for 0%

commit v1 on v0

v1 whole, which is shorter than its diff:
```python
import functools
import math

import jax
import jax.numpy as jnp
from jax import lax
from jax.experimental import pallas as pl
from jax.experimental.pallas import tpu as pltpu
from jax.sharding import PartitionSpec as P

PULSES = 2048
F32 = jnp.float32
BF16 = jnp.bfloat16
TILES = 6
TURN = 1.0 / (2.0 * math.pi)

SIN_POLY = (3.1415926401307086, -5.167710083507905, 2.5500775232148403, -0.5982912856219295, 0.07765766030867731)
COS_POLY = (0.9999999532476086, -4.934792830619651, 4.058411352862725, -1.3318765680816778, 0.21968961109948743)


def horner(q, coefs):
    out = jnp.full_like(q, coefs[-1])
    for c in coefs[-2::-1]:
        out = out * q + c
    return out


def cos_sin_turns(u):
    r = u - jnp.round(u)
    q = r * r
    s = horner(q, SIN_POLY) * r
    c = horner(q, COS_POLY)
    t = s + s
    return 1.0 - t * s, t * c


def iota(shape, dim):
    return lax.broadcasted_iota(jnp.int32, shape, dim)


def kernel(
    fp_hbm, rf_hbm, bb_hbm, vis_hbm, plat_hbm, out_ref,
    fp, rf, bb, vis, plat, pcols, wts, ta, tb, send1, recv1, send2, recv2, recv3, wtab, chirp,
    in_sem, send_sem, recv_sem,
):
    j = lax.axis_index("facet")
    i = lax.axis_index("pulse")
    xl, y, core = j // 8, (j // 2) % 4, j % 2
    xh, z = i // 16, i % 16
    chip_facet = (j // 2) * 2

    ins = [
        pltpu.make_async_copy(src, dst, in_sem.at[n])
        for n, (src, dst) in enumerate(
            ((plat_hbm, plat), (fp_hbm, fp), (bb_hbm, bb), (vis_hbm, vis), (rf_hbm, rf))
        )
    ]
    for c in ins:
        c.start()

    barrier = pltpu.get_barrier_semaphore()
    for t in range(1, 16):
        pl.semaphore_signal(
            barrier, inc=1, device_id={"facet": (j + t) % 16, "pulse": i},
            device_id_type=pl.DeviceIdType.MESH,
        )
    for zs in range(16):
        pl.semaphore_signal(
            barrier, inc=1, device_id={"facet": chip_facet + xh, "pulse": 16 * (1 - core) + zs},
            device_id_type=pl.DeviceIdType.MESH,
        )

    for c in ins:
        c.wait()
    eye = iota((64, 64), 0) == iota((64, 64), 1)
    for d in range(3):
        column = jnp.sum(jnp.where(eye, plat[d : d + 1, :], 0.0), axis=1, keepdims=True)
        pcols[d] = jnp.broadcast_to(column, (64, 128))
    for blk in range(TILES):
        b = bb[blk]
        cols = pl.ds(blk * 128, 128)
        for h in range(2):
            seen = vis[b, h].astype(F32)
            wts[h, :, cols] = rf[:, cols] * seen

    lane = iota((128, 128), 1)
    same_pulse = (iota((128, 128), 0) % 8) == (lane % 8)
    fold = (iota((16, 128), 0) == iota((16, 128), 1) // 8).astype(BF16)
    scale_u = 0.125 * TURN
    for t in range(8):
        tx, ty = 1 - t // 4, (t % 4 + 1) % 4
        g = ((xl + tx) % 2) * 4 + (y + ty) % 4
        rows = pl.ds(pl.multiple_of(g * 8, 8), 8)
        px, py, pz = pcols[0, rows, :], pcols[1, rows, :], pcols[2, rows, :]
        half = g // 4
        buf = t % 2
        for n in range(TILES):
            cols = pl.ds(n * 128, 128)
            dx = fp[0:1, cols] - px
            dy = fp[1:2, cols] - py
            dz = fp[2:3, cols] - pz
            d2 = dx * dx + dy * dy + dz * dz
            u = jnp.sqrt(d2) * scale_u
            w0 = wts[half, 0:1, cols]
            w1 = wts[half, 1:2, cols]
            c0, s0 = cos_sin_turns(u)
            cz, sz = cos_sin_turns(64.0 * u)
            two = 4.0 * (c0 * c0) - 2.0
            cb, sb = [c0], [s0]
            cp, sp = c0, -s0
            for _ in range(15):
                cn, sn = two * cb[-1] - cp, two * sb[-1] - sp
                cp, sp = cb[-1], sb[-1]
                cb.append(cn)
                sb.append(sn)
            arp, aip = w0 * cb[8] - w1 * sb[8], w1 * cb[8] + w0 * sb[8]
            ar = [arp * cz + aip * sz]
            ai = [aip * cz - arp * sz]
            two_z = cz + cz
            for _ in range(15):
                rn, im = two_z * ar[-1] - arp, two_z * ai[-1] - aip
                arp, aip = ar[-1], ai[-1]
                ar.append(rn)
                ai.append(im)
            for m in range(0, 16, 2):
                r16 = slice(m * 8, m * 8 + 16)
                q16 = slice(128 + m * 8, 128 + m * 8 + 16)
                tb[buf, r16, cols] = jnp.concatenate([cb[m], cb[m + 1]], axis=0).astype(BF16)
                tb[buf, q16, cols] = jnp.concatenate([sb[m], sb[m + 1]], axis=0).astype(BF16)
                ta[buf, r16, cols] = jnp.concatenate([ar[m], ar[m + 1]], axis=0).astype(BF16)
                ta[buf, q16, cols] = jnp.concatenate([ai[m], ai[m + 1]], axis=0).astype(BF16)
        prod = lax.dot_general(
            ta[buf], tb[buf], (((1,), (1,)), ((), ())), preferred_element_type=F32
        )
        rc, rs = prod[:128, :128], prod[:128, 128:]
        ic, is_ = prod[128:, :128], prod[128:, 128:]
        parts = []
        for comp in (rc - is_, ic + rs, rc + is_, ic - rs):
            parts.append(jnp.where(same_pulse, comp, 0.0).astype(BF16))
        echo = lax.dot_general(
            fold, jnp.concatenate(parts, axis=1), (((1,), (0,)), ((), ())),
            preferred_element_type=F32,
        )
        for h in range(2):
            for pair in range(2):
                a = echo[8 * h : 8 * h + 8, pair * 256 : pair * 256 + 128]
                b = echo[8 * h : 8 * h + 8, pair * 256 + 128 : pair * 256 + 256]
                send1[t, h, pair * 16 : pair * 16 + 16, :] = jnp.concatenate([a, b], axis=0).astype(BF16)
        if t == 0:
            pl.semaphore_wait(barrier, 31)
        if t < 7:
            for h in range(2):
                pltpu.make_async_remote_copy(
                    src_ref=send1.at[t, h], dst_ref=recv1.at[2 * t + core],
                    send_sem=send_sem.at[0], recv_sem=recv_sem.at[0],
                    device_id={"facet": g * 2 + h, "pulse": i},
                    device_id_type=pl.DeviceIdType.MESH,
                ).start()
        else:
            pltpu.make_async_remote_copy(
                src_ref=send1.at[7, 1 - core], dst_ref=recv1.at[14],
                send_sem=send_sem.at[0], recv_sem=recv_sem.at[0],
                device_id={"facet": g * 2 + 1 - core, "pulse": i},
                device_id_type=pl.DeviceIdType.MESH,
            ).start()

    lanes = iota((1, 512), 1)
    owner = (j + 1 + lanes // 32) % 16
    first = 64 * (16 * (1 - owner % 2) + lanes % 16) + 8 * (owner // 2) + 4 * (lanes // 16 % 2)
    first = first.astype(F32)
    norm = 1.0 / math.sqrt(PULSES)

    def weight_rows(m, carry):
        k = (j * 128 + m * 16 + iota((16, 512), 0)).astype(F32)
        wr, wi = cos_sin_turns(k * first * (1.0 / PULSES))
        wr, wi = wr * norm, -wi * norm
        er, ei = cos_sin_turns(k * (1.0 / PULSES))
        rows = pl.ds(pl.multiple_of(m * 16, 16), 16)
        rows_i = pl.ds(pl.multiple_of(128 + m * 16, 16), 16)
        for q in range(4):
            wtab[q, rows, :] = wr.astype(BF16)
            wtab[q, rows_i, :] = wi.astype(BF16)
            wr, wi = wr * er + wi * ei, wi * er - wr * ei
        return carry

    lax.fori_loop(0, 8, weight_rows, 0)

    row = iota((256, 256), 0)
    col = iota((256, 256), 1)
    comp_r, bin_r, pulse_r = row // 128, row // 8 % 16, row % 8
    comp_c, bin_c, pulse_c = col // 16 % 2, col % 16, col // 32
    same = jnp.logical_and(comp_r == comp_c, pulse_r == pulse_c)
    turn_up = jnp.where(jnp.logical_and(same, bin_r == bin_c), 1.0, 0.0).astype(BF16)
    turn_down = jnp.where(jnp.logical_and(same, bin_r == 15 - bin_c), 1.0, 0.0).astype(BF16)

    got1 = pltpu.make_async_remote_copy(
        src_ref=recv1, dst_ref=recv1, send_sem=send_sem.at[0], recv_sem=recv_sem.at[0],
        device_id={"facet": j, "pulse": i}, device_id_type=pl.DeviceIdType.MESH,
    )
    got1.wait_recv()
    total = send1[7, core].astype(F32)
    for s in range(15):
        total = total + recv1[s].astype(F32)
    for sign, turn in ((0, turn_down), (1, turn_up)):
        lo = sign * 16
        pieces = jnp.concatenate([total[lo : lo + 8], total[lo + 8 : lo + 16]], axis=1).astype(BF16)
        turned = jnp.dot(pieces, turn, preferred_element_type=F32)
        for a in range(8):
            for ph in range(2):
                send2[2 * a + sign, ph : ph + 1, :] = turned[a : a + 1, ph * 128 : ph * 128 + 128]
    for t in range(16):
        zd = (z + t) % 16
        pltpu.make_async_remote_copy(
            src_ref=send2.at[zd], dst_ref=recv2.at[z],
            send_sem=send_sem.at[1], recv_sem=recv_sem.at[1],
            device_id={"facet": chip_facet + 1 - xh, "pulse": 16 * core + zd},
            device_id_type=pl.DeviceIdType.MESH,
        ).start()

    kk = (j * 128 - PULSES // 2 + iota((16, 128), 1)).astype(F32)
    ff = (i * 16 + iota((16, 128), 0)).astype(F32)
    ch_c, ch_s = cos_sin_turns(kk * kk * (1.0 / PULSES) / (2.0 + 0.25 * ff))
    chirp[0] = ch_c
    chirp[1] = ch_s

    got2 = pltpu.make_async_remote_copy(
        src_ref=send2, dst_ref=recv2, send_sem=send_sem.at[1], recv_sem=recv_sem.at[1],
        device_id={"facet": j, "pulse": i}, device_id_type=pl.DeviceIdType.MESH,
    )
    got2.wait_recv()
    recv3[15] = jnp.concatenate([recv2[:, 0, :], recv2[:, 1, :]], axis=0).astype(BF16)
    for t in range(1, 16):
        pltpu.make_async_remote_copy(
            src_ref=recv3.at[15], dst_ref=recv3.at[15 - t],
            send_sem=send_sem.at[2], recv_sem=recv_sem.at[2],
            device_id={"facet": (j + t) % 16, "pulse": i},
            device_id_type=pl.DeviceIdType.MESH,
        ).start()
    got3 = pltpu.make_async_remote_copy(
        src_ref=recv3.at[pl.ds(0, 15)], dst_ref=recv3.at[pl.ds(0, 15)],
        send_sem=send_sem.at[2], recv_sem=recv_sem.at[2],
        device_id={"facet": j, "pulse": i}, device_id_type=pl.DeviceIdType.MESH,
    )
    got3.wait_recv()

    held = recv3[...].reshape(512, 128)
    slot = iota((256, 128), 1) // 32
    acc = jnp.zeros((256, 128), F32)
    for q in range(4):
        full = jnp.dot(wtab[q], held, preferred_element_type=F32)
        acc = jnp.where(slot == q, full, acc)
    flat = acc.T
    summed = flat[0:32] + flat[32:64] + flat[64:96] + flat[96:128]
    re = summed[0:16, 0:128] - summed[16:32, 128:256]
    im = summed[0:16, 128:256] + summed[16:32, 0:128]
    out_ref[0] = chirp[0] * re - chirp[1] * im
    out_ref[1] = chirp[0] * im + chirp[1] * re

    got1.wait_send()
    got2.wait_send()
    got3.wait_send()


def body(facet_positions, reflectivity, block_building, visible, platform):
    anywhere = pl.BlockSpec(memory_space=pl.ANY)
    return pl.pallas_call(
        kernel,
        out_shape=jax.ShapeDtypeStruct((2, 16, 128), F32),
        in_specs=[anywhere] * 5,
        out_specs=pl.BlockSpec(memory_space=pltpu.VMEM),
        scratch_shapes=[
            pltpu.VMEM((3, 768), F32),
            pltpu.VMEM((2, 768), F32),
            pltpu.SMEM((6,), jnp.int32),
            pltpu.SMEM((24, 2), jnp.int32),
            pltpu.VMEM((3, 64), F32),
            pltpu.VMEM((3, 64, 128), F32),
            pltpu.VMEM((2, 2, 768), F32),
            pltpu.VMEM((2, 256, 768), BF16),
            pltpu.VMEM((2, 256, 768), BF16),
            pltpu.VMEM((8, 2, 32, 128), BF16),
            pltpu.VMEM((15, 32, 128), BF16),
            pltpu.VMEM((16, 2, 128), F32),
            pltpu.VMEM((16, 2, 128), F32),
            pltpu.VMEM((16, 32, 128), BF16),
            pltpu.VMEM((4, 256, 512), BF16),
            pltpu.VMEM((2, 16, 128), F32),
            pltpu.SemaphoreType.DMA((5,)),
            pltpu.SemaphoreType.DMA((3,)),
            pltpu.SemaphoreType.DMA((3,)),
        ],
        compiler_params=pltpu.CompilerParams(
            collective_id=0, has_side_effects=True, vmem_limit_bytes=32 * 1024 * 1024
        ),
    )(facet_positions, reflectivity, block_building, visible, platform)


def solution(mesh):
    return jax.shard_map(
        body,
        mesh=mesh,
        in_specs=(P(None, "facet"), P(None, "facet"), P("facet"), P(None, "pulse"), P(None, "pulse")),
        out_specs=P(None, "pulse", "facet"),
        check_vma=False,
    )
```

time: 139 us -> 39.7 us (0.29)
  other arithmetic: 43.1 us -> 0 us
  Pallas kernels: 0 us -> 36.7 us
  starting transfers between devices: 32.8 us -> 0 us
  waiting for transfers between devices: 29.9 us -> 0 us
  matrix products: 19.8 us -> 0 us
  local copies, waits for them, and re-layouts: 11.3 us -> 2.77 us
    another operation x33 -> x0, other arithmetic: 38.7 us -> none
    pallas_call x0 -> x1, Pallas kernels: none -> 36.7 us  [body(): pl.pallas_call(kernel, out_shape=jax.ShapeDtypeStruct((2, 16, 128), F32),...]
    all_to_all x4 -> x0, starting transfers between devices: 32.8 us -> none  [the longest x2 17.5 us: from_everyone(): return lax.all_to_all(copies, axis, split_axis=0, concat_axis=0, tiled=True)]
    all_to_all x4 -> x0, waiting for transfers between devices: 29.9 us -> none  [the longest x2 15.3 us: exchange_in_order(): lax.all_to_all(pieces, axes[k], split_axis=k, concat_axis=k, tiled=True)]
    dot_general x20 -> x0, matrix products: 19.8 us -> none  [the longest x4 16.3 us: contract(): lax.dot_general(left_side, right_side, (((1,), (1,)), ((), ())), preferre...]
    another operation x32 -> x0, local copies, waits for them, and re-layouts: 2.64 us -> none  [echo_group(): return jnp.stack([real_part, imag_part]).reshape(2, antenna.shape[1], BINS)]
    slice x35 -> x0, local copies, waits for them, and re-layouts: 1.84 us -> none  [the longest x16 1.58 us: echo_group(): weights[0][None, None, :] * cosine + weights[1][None, None, :] * sine_a]
    sub x16 -> x0, other arithmetic: 1.54 us -> none  [echo_group(): real_part = products[:, :BIN_HI, :BIN_LO] - products[:, BIN_HI:, BIN_LO:]]
  transfers between devices with their start and end apart: 4 -> 0, of which waited for: 4 -> 0; matrix products, arithmetic and copies ran while one was open for 0% -> 0% of each run, Pallas kernels for 0% -> 0%
where the time goes in v1:
time: 39.7 us; the launch traced here: 39.5 us
  Pallas kernels  36.7 us (92%)
  local copies, waits for them, and re-layouts  2.77 us (7%)
    pallas_call x1, Pallas kernels, body(): pl.pallas_call(kernel, out_shape=jax.ShapeDtypeStruct((2, 16, 128), F32),...  36.7 us
    unnamed x10, local copies, waits for them, and re-layouts  2.77 us

profile of v1, /device:TPU:1, one launch (start us, length us, event | category | flops | bytes accessed | tf_op | source)
XLA Modules:
  0.0 39.5 jit_solution(15557149248324285558)
XLA Ops:
  0.0 0.0 copy-start.3
  0.0 0.0 copy-start
  0.0 0.8 %copy.6.vis_hbm = s32[24,2]{1,0:T(8,128)S(1)} copy(s32[24,2]{0,1:T(2,128)} %param.8) | data formatting | bytes 384 | tf_op args[3]
  0.8 0.0 copy-done.3
  0.8 0.0 copy-done
  0.8 0.0 copy-start.1
  0.8 0.7 %copy-done.1 = f32[2,768]{1,0:T(2,128)S(1)} copy-done((f32[2,768]{1,0:T(2,128)S(1)}, f32[2,768]{1,0:T(2,128)}, u32[]{:S(2)}) %copy-start.1) | copy-done | bytes 6168
  1.5 0.0 copy-start.2
  1.5 0.7 %copy-done.2 = f32[3,64]{1,0:T(4,128)S(1)} copy-done((f32[3,64]{1,0:T(4,128)S(1)}, f32[3,64]{1,0:T(4,128)}, u32[]{:S(2)}) %copy-start.2) | copy-done | bytes 792
  2.2 36.7 %shard_map.55 = f32[2,16,128]{2,1,0:T(8,128)S(1)} custom-call(f32[3,768]{1,0:T(4,128)S(1)} %copy-done, f32[2,768]{1,0:T(2,128)S(1)} %copy-done.1, s32[6]{0:T(128)S(1)} %copy-done.3, s32[24,2]{1,0:T(8,128)S(1)} %copy.6.vis_hbm, f32[3,64]{1,0:T(4,128)S(1)} %copy-done.2), custom_call_target="tpu_custom_call" | custom-call | tf_op jit(solution)/shard_map/pallas_call | solution.py:266
  38.8 0.6 %copy.8 = f32[2,16,128]{2,1,0:T(8,128)} copy(f32[2,16,128]{2,1,0:T(8,128)S(1)} %shard_map.55) | data formatting | bytes 32768
Async XLA Ops:
  0.0 0.8 %copy-start.3 = (s32[6]{0:T(128)S(1)}, s32[6]{0:T(128)}, u32[]{:S(2)}) copy-start(s32[6]{0:T(128)} %bb_hbm.1) | copy-start | bytes 76
  0.0 0.8 %copy-start = (f32[3,768]{1,0:T(4,128)S(1)}, f32[3,768]{1,0:T(4,128)}, u32[]{:S(2)}) copy-start(f32[3,768]{1,0:T(4,128)} %fp_hbm.1) | copy-start | bytes 27652
  0.8 0.7 %copy-start.1 = (f32[2,768]{1,0:T(2,128)S(1)}, f32[2,768]{1,0:T(2,128)}, u32[]{:S(2)}) copy-start(f32[2,768]{1,0:T(2,128)} %rf_hbm.1) | copy-start | bytes 18436
  1.5 0.7 %copy-start.2 = (f32[3,64]{1,0:T(4,128)S(1)}, f32[3,64]{1,0:T(4,128)}, u32[]{:S(2)}) copy-start(f32[3,64]{1,0:T(4,128)} %plat_hbm.1) | copy-start | bytes 2308

commit v2 on v1

v2 whole, which is shorter than its diff:
```python
import functools
import math

import jax
import jax.numpy as jnp
from jax import lax
from jax.experimental import pallas as pl
from jax.experimental.pallas import tpu as pltpu
from jax.sharding import PartitionSpec as P

PULSES = 2048
F32 = jnp.float32
BF16 = jnp.bfloat16
TILES = 6
TURN = 1.0 / (2.0 * math.pi)

SIN_POLY = (3.1415926401307086, -5.167710083507905, 2.5500775232148403, -0.5982912856219295, 0.07765766030867731)
COS_POLY = (0.9999999532476086, -4.934792830619651, 4.058411352862725, -1.3318765680816778, 0.21968961109948743)


def horner(q, coefs):
    out = jnp.full_like(q, coefs[-1])
    for c in coefs[-2::-1]:
        out = out * q + c
    return out


def cos_sin_turns(u):
    r = u - jnp.round(u)
    q = r * r
    s = horner(q, SIN_POLY) * r
    c = horner(q, COS_POLY)
    t = s + s
    return 1.0 - t * s, t * c


def iota(shape, dim):
    return lax.broadcasted_iota(jnp.int32, shape, dim)


def kernel(
    fp_hbm, rf_hbm, bb_hbm, vis_hbm, plat_hbm, out_ref,
    fp, rf, bb, vis, plat, pcols, wts, ta, tb, own, send0, recv0, send2, recv2, send3, recv3,
    tdft, twid, vdft, chirp, in_sem, send_sem, recv_sem,
):
    j = lax.axis_index("facet")
    i = lax.axis_index("pulse")
    chip, core = j // 2, j % 2
    xh, z = i // 16, i % 16
    sibling = {"facet": chip * 2 + 1 - core, "pulse": i}

    ins = [
        pltpu.make_async_copy(src, dst, in_sem.at[n])
        for n, (src, dst) in enumerate(
            ((plat_hbm, plat), (fp_hbm, fp), (bb_hbm, bb), (vis_hbm, vis), (rf_hbm, rf))
        )
    ]
    for c in ins:
        c.start()

    def remote(src, dst, k, device):
        return pltpu.make_async_remote_copy(
            src_ref=src, dst_ref=dst, send_sem=send_sem.at[k], recv_sem=recv_sem.at[k],
            device_id=device, device_id_type=pl.DeviceIdType.MESH,
        )

    barrier = pltpu.get_barrier_semaphore()

    def greet(device):
        pl.semaphore_signal(
            barrier, inc=1, device_id=device, device_id_type=pl.DeviceIdType.MESH
        )

    for t in (8, 7, 9, 6, 10, 5, 11, 4, 12, 3, 13, 2, 14, 1, 15):
        greet({"facet": j, "pulse": 16 * xh + (z + t) % 16})
    for r in (1, 0):
        for t in range(7, -1, -1):
            source = {"facet": (chip + t) % 8 * 2 + xh, "pulse": 16 * ((xh + r) % 2) + z}
            if t or r:
                greet(source)
            else:
                pl.when(core != xh)(functools.partial(greet, source))
    greet(sibling)

    for c in ins:
        c.wait()
    eye = iota((64, 64), 0) == iota((64, 64), 1)
    for d in range(3):
        column = jnp.sum(jnp.where(eye, plat[d : d + 1, :], 0.0), axis=1, keepdims=True)
        pcols[d] = jnp.broadcast_to(column, (64, 128))
    for blk in range(TILES):
        b = bb[blk]
        cols = pl.ds(blk * 128, 128)
        for h in range(2):
            seen = vis[h, b].astype(F32)
            wts[h, :, cols] = rf[:, cols] * seen

    lane = iota((128, 128), 1)
    same_pulse = (iota((128, 128), 0) % 8) == (lane % 8)
    fold = (iota((16, 128), 0) == iota((16, 128), 1) // 8).astype(BF16)
    scale_u = 0.125 * TURN
    for g in range(8):
        rows = slice(g * 8, g * 8 + 8)
        px, py, pz = pcols[0, rows, :], pcols[1, rows, :], pcols[2, rows, :]
        half = g // 4
        buf = g % 2
        for n in range(TILES):
            cols = pl.ds(n * 128, 128)
            dx = fp[0:1, cols] - px
            dy = fp[1:2, cols] - py
            dz = fp[2:3, cols] - pz
            d2 = dx * dx + dy * dy + dz * dz
            u = jnp.sqrt(d2) * scale_u
            w0 = wts[half, 0:1, cols]
            w1 = wts[half, 1:2, cols]
            c0, s0 = cos_sin_turns(u)
            cz, sz = cos_sin_turns(64.0 * u)
            two = 4.0 * (c0 * c0) - 2.0
            cb, sb = [c0], [s0]
            cp, sp = c0, -s0
            for _ in range(15):
                cn, sn = two * cb[-1] - cp, two * sb[-1] - sp
                cp, sp = cb[-1], sb[-1]
                cb.append(cn)
                sb.append(sn)
            arp, aip = w0 * cb[8] - w1 * sb[8], w1 * cb[8] + w0 * sb[8]
            ar = [arp * cz + aip * sz]
            ai = [aip * cz - arp * sz]
            two_z = cz + cz
            for _ in range(15):
                rn, im = two_z * ar[-1] - arp, two_z * ai[-1] - aip
                arp, aip = ar[-1], ai[-1]
                ar.append(rn)
                ai.append(im)
            for m in range(0, 16, 2):
                r16 = slice(m * 8, m * 8 + 16)
                q16 = slice(128 + m * 8, 128 + m * 8 + 16)
                tb[buf, r16, cols] = jnp.concatenate([cb[m], cb[m + 1]], axis=0).astype(BF16)
                tb[buf, q16, cols] = jnp.concatenate([sb[m], sb[m + 1]], axis=0).astype(BF16)
                ta[buf, r16, cols] = jnp.concatenate([ar[m], ar[m + 1]], axis=0).astype(BF16)
                ta[buf, q16, cols] = jnp.concatenate([ai[m], ai[m + 1]], axis=0).astype(BF16)
        prod = lax.dot_general(
            ta[buf], tb[buf], (((1,), (1,)), ((), ())), preferred_element_type=F32
        )
        rc, rs = prod[:128, :128], prod[:128, 128:]
        ic, is_ = prod[128:, :128], prod[128:, 128:]
        parts = []
        for comp in (rc - is_, ic + rs, rc + is_, ic - rs):
            parts.append(jnp.where(same_pulse, comp, 0.0).astype(BF16))
        echo = lax.dot_general(
            fold, jnp.concatenate(parts, axis=1), (((1,), (0,)), ((), ())),
            preferred_element_type=F32,
        )
        mine = jnp.where(core == 0, echo[:8], echo[8:])
        other = jnp.where(core == 0, echo[8:], echo[:8])
        for comp in range(4):
            own[g * 32 + comp * 8 : g * 32 + comp * 8 + 8, :] = mine[:, comp * 128 : comp * 128 + 128]
        for pair in range(2):
            a = other[:, pair * 256 : pair * 256 + 128]
            b = other[:, pair * 256 + 128 : pair * 256 + 256]
            send0[g, pair * 16 : pair * 16 + 16, :] = jnp.concatenate([a, b], axis=0).astype(BF16)

    lanes = iota((16, 256), 1)
    pulse8 = (8 * (16 * xh + (z + 1 + lanes // 16) % 16) + lanes % 8).astype(F32)
    real_col = lanes // 8 % 2 == 0

    def dft_rows(m, carry):
        k = (m * 16 + iota((16, 256), 0)).astype(F32)
        c, s = cos_sin_turns(k * pulse8 * (1.0 / 256.0))
        rows = pl.ds(pl.multiple_of(m * 16, 16), 16)
        rows_i = pl.ds(pl.multiple_of(256 + m * 16, 16), 16)
        tdft[rows, :] = jnp.where(real_col, c, s).astype(BF16)
        tdft[rows_i, :] = jnp.where(real_col, -s, c).astype(BF16)
        kt = (m * 16 + iota((16, 128), 0)).astype(F32)
        pt = (iota((16, 128), 1) % 8).astype(F32)
        c, s = cos_sin_turns(kt * pt * (1.0 / PULSES))
        twid[0, rows, :] = c
        twid[1, rows, :] = s
        return carry

    lax.fori_loop(0, 16, dft_rows, 0)

    row = iota((16, 256), 0)
    col = iota((16, 256), 1)
    bin_here = jnp.where(z % 2 == 1, row, 15 - row)
    same_bin = col // 8 % 16 == bin_here
    for h in range(8):
        c, s = cos_sin_turns((h * (col % 8)).astype(F32) * 0.125)
        first = col < 128
        vdft[h * 16 : h * 16 + 16, :] = jnp.where(same_bin, jnp.where(first, c, s), 0.0).astype(BF16)
        vdft[128 + h * 16 : 144 + h * 16, :] = jnp.where(
            same_bin, jnp.where(first, -s, c), 0.0
        ).astype(BF16)

    kk = (j * 128 - PULSES // 2 + iota((16, 128), 1)).astype(F32)
    ff = (i * 16 + iota((16, 128), 0)).astype(F32)
    ch_c, ch_s = cos_sin_turns(kk * kk * (1.0 / PULSES) / (2.0 + 0.25 * ff))
    chirp[0] = ch_c * (1.0 / math.sqrt(PULSES))
    chirp[1] = ch_s * (1.0 / math.sqrt(PULSES))

    pl.semaphore_wait(barrier, jnp.where(core == xh, 31, 32))

    pair_copy = remote(send0, recv0, 0, sibling)
    pair_copy.start()
    pair_copy.wait_recv()
    for g in range(8):
        rows = slice(g * 32, g * 32 + 32)
        own[rows, :] = own[rows, :] + recv0[g].astype(F32)

    for a in range(8):
        for sign in range(2):
            piece = [own[pl.ds(sign * 16 + c * 8 + a, 8, stride=32), :] for c in range(2)]
            send2[2 * a + sign] = jnp.concatenate(piece, axis=0).astype(BF16)
    for t in (8, 7, 9, 6, 10, 5, 11, 4, 12, 3, 13, 2, 14, 1, 15):
        zd = (z + t) % 16
        remote(send2.at[zd], recv2.at[15 - t], 1, {"facet": j, "pulse": 16 * xh + zd}).start()
    recv2[15] = send2[z]
    first15 = recv2.at[pl.ds(0, 15)]
    got2 = remote(first15, first15, 1, sibling)
    got2.wait_recv()

    held = recv2[...].reshape(256, 128)
    low = jnp.dot(tdft[...], held, preferred_element_type=F32)
    lr, li = low[:256], low[256:]
    tr, ts = twid[0], twid[1]
    turned = jnp.concatenate([lr * tr + li * ts, li * tr - lr * ts], axis=1).astype(BF16)
    spec = lax.dot_general(
        vdft[...], turned, (((1,), (1,)), ((), ())), preferred_element_type=F32
    )
    for h in range(8):
        for odd in range(2):
            cols = slice(odd * 128, odd * 128 + 128)
            send3[2 * h + odd] = jnp.concatenate(
                [spec[h * 16 : h * 16 + 16, cols], spec[128 + h * 16 : 144 + h * 16, cols]], axis=0
            ).astype(BF16)

    place = recv3.at[8 * xh + chip]
    to_self = core == xh
    for t in range(15, 0, -1):
        jd = (j + t) % 16
        remote(send3.at[jd], place, 2, {"facet": jd, "pulse": 16 * core + z}).start()

    @pl.when(to_self)
    def _():
        pltpu.make_async_copy(send3.at[j], place, recv_sem.at[2]).start()

    @pl.when(jnp.logical_not(to_self))
    def _():
        remote(send3.at[j], place, 2, {"facet": j, "pulse": 16 * core + z}).start()

    got3 = remote(send3, recv3, 2, sibling)
    got3.wait_recv()
    total = recv3[0].astype(F32)
    for n in range(1, 16):
        total = total + recv3[n].astype(F32)
    re, im = total[:16], total[16:]
    out_ref[0] = chirp[0] * re - chirp[1] * im
    out_ref[1] = chirp[0] * im + chirp[1] * re

    pair_copy.wait_send()
    got2.wait_send()

    @pl.when(to_self)
    def _():
        most = send3.at[pl.ds(0, 15)]
        remote(most, most, 2, sibling).wait_send()

    @pl.when(jnp.logical_not(to_self))
    def _():
        got3.wait_send()


def body(facet_positions, reflectivity, block_building, visible, platform):
    anywhere = pl.BlockSpec(memory_space=pltpu.HBM)
    return pl.pallas_call(
        kernel,
        out_shape=jax.ShapeDtypeStruct((2, 16, 128), F32),
        in_specs=[anywhere] * 5,
        out_specs=pl.BlockSpec(memory_space=pltpu.VMEM),
        scratch_shapes=[
            pltpu.VMEM((3, 768), F32),
            pltpu.VMEM((2, 768), F32),
            pltpu.SMEM((6,), jnp.int32),
            pltpu.SMEM((2, 24), jnp.int32),
            pltpu.VMEM((3, 64), F32),
            pltpu.VMEM((3, 64, 128), F32),
            pltpu.VMEM((2, 2, 768), F32),
            pltpu.VMEM((2, 256, 768), BF16),
            pltpu.VMEM((2, 256, 768), BF16),
            pltpu.VMEM((256, 128), F32),
            pltpu.VMEM((8, 32, 128), BF16),
            pltpu.VMEM((8, 32, 128), BF16),
            pltpu.VMEM((16, 16, 128), BF16),
            pltpu.VMEM((16, 16, 128), BF16),
            pltpu.VMEM((16, 32, 128), BF16),
            pltpu.VMEM((16, 32, 128), BF16),
            pltpu.VMEM((512, 256), BF16),
            pltpu.VMEM((2, 256, 128), F32),
            pltpu.VMEM((256, 256), BF16),
            pltpu.VMEM((2, 16, 128), F32),
            pltpu.SemaphoreType.DMA((5,)),
            pltpu.SemaphoreType.DMA((3,)),
            pltpu.SemaphoreType.DMA((3,)),
        ],
        compiler_params=pltpu.CompilerParams(
            collective_id=0, has_side_effects=True, vmem_limit_bytes=62 * 1024 * 1024
        ),
    )(facet_positions, reflectivity, block_building, visible.T, platform)


def solution(mesh):
    return jax.shard_map(
        body,
        mesh=mesh,
        in_specs=(P(None, "facet"), P(None, "facet"), P("facet"), P(None, "pulse"), P(None, "pulse")),
        out_specs=P(None, "pulse", "facet"),
        check_vma=False,
    )
```

time: 39.7 us -> 33.5 us (0.84)
  Pallas kernels: 36.7 us -> 32 us
  local copies, waits for them, and re-layouts: 2.77 us -> 1.32 us
    pallas_call x1, Pallas kernels: 36.7 us -> 32 us  [body(): pl.pallas_call(kernel, out_shape=jax.ShapeDtypeStruct((2, 16, 128), F32),...]
    unnamed x10 -> x1, local copies, waits for them, and re-layouts: 2.77 us -> 1.32 us
where the time goes in v2:
time: 33.5 us; the launch traced here: 33.3 us
  Pallas kernels  32 us (96%)
  local copies, waits for them, and re-layouts  1.32 us (4%)
    pallas_call x1, Pallas kernels, body(): pl.pallas_call(kernel, out_shape=jax.ShapeDtypeStruct((2, 16, 128), F32),...  32 us
    unnamed x1, local copies, waits for them, and re-layouts  1.32 us

profile of v2, /device:TPU:1, one launch (start us, length us, event | category | flops | bytes accessed | tf_op | source)
XLA Modules:
  0.0 33.3 jit_solution(12632612178447067449)
XLA Ops:
  0.0 32.0 %shard_map.55 = f32[2,16,128]{2,1,0:T(8,128)} custom-call(f32[3,768]{1,0:T(4,128)} %fp_hbm.1, f32[2,768]{1,0:T(2,128)} %rf_hbm.1, s32[6]{0:T(128)} %bb_hbm.1, s32[2,24]{1,0:T(2,128)} %bitcast.1, f32[3,64]{1,0:T(4,128)} %plat_hbm.1), custom_call_target="tpu_custom_call" | custom-call | tf_op jit(solution)/shard_map/pallas_call | solution.py:275
  32.0 1.3 %copy.7 = f32[2,16,128]{2,1,0:T(8,128)} copy(f32[2,16,128]{2,1,0:T(8,128)} %shard_map.55) | data formatting | bytes 32768

commit v3 on v2

--- a/solution.py
+++ b/solution.py
@@ -41,22 +41,13 @@
 def kernel(
     fp_hbm, rf_hbm, bb_hbm, vis_hbm, plat_hbm, out_ref,
     fp, rf, bb, vis, plat, pcols, wts, ta, tb, own, send0, recv0, send2, recv2, send3, recv3,
-    tdft, twid, vdft, chirp, in_sem, send_sem, recv_sem,
+    tdft, twid, vdft, chirp, prods, masked, in_sem, send_sem, recv_sem,
 ):
     j = lax.axis_index("facet")
     i = lax.axis_index("pulse")
     chip, core = j // 2, j % 2
     xh, z = i // 16, i % 16
     sibling = {"facet": chip * 2 + 1 - core, "pulse": i}
-
-    ins = [
-        pltpu.make_async_copy(src, dst, in_sem.at[n])
-        for n, (src, dst) in enumerate(
-            ((plat_hbm, plat), (fp_hbm, fp), (bb_hbm, bb), (vis_hbm, vis), (rf_hbm, rf))
-        )
-    ]
-    for c in ins:
-        c.start()
 
     def remote(src, dst, k, device):
         return pltpu.make_async_remote_copy(
@@ -81,6 +72,53 @@
             else:
                 pl.when(core != xh)(functools.partial(greet, source))
     greet(sibling)
+
+    ins = [
+        pltpu.make_async_copy(src, dst, in_sem.at[n])
+        for n, (src, dst) in enumerate(
+            ((plat_hbm, plat), (fp_hbm, fp), (bb_hbm, bb), (vis_hbm, vis), (rf_hbm, rf))
+        )
+    ]
+    for c in ins:
+        c.start()
+
+    lanes = iota((16, 256), 1)
+    pulse8 = (8 * (16 * xh + (z + 1 + lanes // 16) % 16) + lanes % 8).astype(F32)
+    real_col = lanes // 8 % 2 == 0
+
+    def dft_rows(m, carry):
+        k = (m * 16 + iota((16, 256), 0)).astype(F32)
+        c, s = cos_sin_turns(k * pulse8 * (1.0 / 256.0))
+        rows = pl.ds(pl.multiple_of(m * 16, 16), 16)
+        rows_i = pl.ds(pl.multiple_of(256 + m * 16, 16), 16)
+        tdft[rows, :] = jnp.where(real_col, c, s).astype(BF16)
+        tdft[rows_i, :] = jnp.where(real_col, -s, c).astype(BF16)
+        kt = (m * 16 + iota((16, 128), 0)).astype(F32)
+        pt = (iota((16, 128), 1) % 8).astype(F32)
+        c, s = cos_sin_turns(kt * pt * (1.0 / PULSES))
+        twid[0, rows, :] = c
+        twid[1, rows, :] = s
+        return carry
+
+    lax.fori_loop(0, 16, dft_rows, 0)
+
+    row = iota((16, 256), 0)
+    col = iota((16, 256), 1)
+    bin_here = jnp.where(z % 2 == 1, row, 15 - row)
+    same_bin = col // 8 % 16 == bin_here
+    for h in range(8):
+        c, s = cos_sin_turns((h * (col % 8)).astype(F32) * 0.125)
+        first = col < 128
+        vdft[h * 16 : h * 16 + 16, :] = jnp.where(same_bin, jnp.where(first, c, s), 0.0).astype(BF16)
+        vdft[128 + h * 16 : 144 + h * 16, :] = jnp.where(
+            same_bin, jnp.where(first, -s, c), 0.0
+        ).astype(BF16)
+
+    kk = (j * 128 - PULSES // 2 + iota((16, 128), 1)).astype(F32)
+    ff = (i * 16 + iota((16, 128), 0)).astype(F32)
+    ch_c, ch_s = cos_sin_turns(kk * kk * (1.0 / PULSES) / (2.0 + 0.25 * ff))
+    chirp[0] = ch_c * (1.0 / math.sqrt(PULSES))
+    chirp[1] = ch_s * (1.0 / math.sqrt(PULSES))
 
     for c in ins:
         c.wait()
@@ -99,7 +137,7 @@
     same_pulse = (iota((128, 128), 0) % 8) == (lane % 8)
     fold = (iota((16, 128), 0) == iota((16, 128), 1) // 8).astype(BF16)
     scale_u = 0.125 * TURN
-    for g in range(8):
+    def make_tables(g):
         rows = slice(g * 8, g * 8 + 8)
         px, py, pz = pcols[0, rows, :], pcols[1, rows, :], pcols[2, rows, :]
         half = g // 4
@@ -139,16 +177,24 @@
                 tb[buf, q16, cols] = jnp.concatenate([sb[m], sb[m + 1]], axis=0).astype(BF16)
                 ta[buf, r16, cols] = jnp.concatenate([ar[m], ar[m + 1]], axis=0).astype(BF16)
                 ta[buf, q16, cols] = jnp.concatenate([ai[m], ai[m + 1]], axis=0).astype(BF16)
-        prod = lax.dot_general(
+
+    def products(g):
+        buf = g % 2
+        return lax.dot_general(
             ta[buf], tb[buf], (((1,), (1,)), ((), ())), preferred_element_type=F32
         )
+
+    def kept(prod):
         rc, rs = prod[:128, :128], prod[:128, 128:]
         ic, is_ = prod[128:, :128], prod[128:, 128:]
         parts = []
         for comp in (rc - is_, ic + rs, rc + is_, ic - rs):
             parts.append(jnp.where(same_pulse, comp, 0.0).astype(BF16))
+        return jnp.concatenate(parts, axis=1)
+
+    def fold_up(g, parts):
         echo = lax.dot_general(
-            fold, jnp.concatenate(parts, axis=1), (((1,), (0,)), ((), ())),
+            fold, parts, (((1,), (0,)), ((), ())),
             preferred_element_type=F32,
         )
         mine = jnp.where(core == 0, echo[:8], echo[8:])
@@ -160,43 +206,17 @@
             b = other[:, pair * 256 + 128 : pair * 256 + 256]
             send0[g, pair * 16 : pair * 16 + 16, :] = jnp.concatenate([a, b], axis=0).astype(BF16)
 
-    lanes = iota((16, 256), 1)
-    pulse8 = (8 * (16 * xh + (z + 1 + lanes // 16) % 16) + lanes % 8).astype(F32)
-    real_col = lanes // 8 % 2 == 0
-
-    def dft_rows(m, carry):
-        k = (m * 16 + iota((16, 256), 0)).astype(F32)
-        c, s = cos_sin_turns(k * pulse8 * (1.0 / 256.0))
-        rows = pl.ds(pl.multiple_of(m * 16, 16), 16)
-        rows_i = pl.ds(pl.multiple_of(256 + m * 16, 16), 16)
-        tdft[rows, :] = jnp.where(real_col, c, s).astype(BF16)
-        tdft[rows_i, :] = jnp.where(real_col, -s, c).astype(BF16)
-        kt = (m * 16 + iota((16, 128), 0)).astype(F32)
-        pt = (iota((16, 128), 1) % 8).astype(F32)
-        c, s = cos_sin_turns(kt * pt * (1.0 / PULSES))
-        twid[0, rows, :] = c
-        twid[1, rows, :] = s
-        return carry
-
-    lax.fori_loop(0, 16, dft_rows, 0)
-
-    row = iota((16, 256), 0)
-    col = iota((16, 256), 1)
-    bin_here = jnp.where(z % 2 == 1, row, 15 - row)
-    same_bin = col // 8 % 16 == bin_here
-    for h in range(8):
-        c, s = cos_sin_turns((h * (col % 8)).astype(F32) * 0.125)
-        first = col < 128
-        vdft[h * 16 : h * 16 + 16, :] = jnp.where(same_bin, jnp.where(first, c, s), 0.0).astype(BF16)
-        vdft[128 + h * 16 : 144 + h * 16, :] = jnp.where(
-            same_bin, jnp.where(first, -s, c), 0.0
-        ).astype(BF16)
-
-    kk = (j * 128 - PULSES // 2 + iota((16, 128), 1)).astype(F32)
-    ff = (i * 16 + iota((16, 128), 0)).astype(F32)
-    ch_c, ch_s = cos_sin_turns(kk * kk * (1.0 / PULSES) / (2.0 + 0.25 * ff))
-    chirp[0] = ch_c * (1.0 / math.sqrt(PULSES))
-    chirp[1] = ch_s * (1.0 / math.sqrt(PULSES))
+
+    make_tables(0)
+    for g in range(9):
+        if g < 8:
+            prods[g % 2] = products(g)
+        if g < 7:
+            make_tables(g + 1)
+        if g > 0:
+            fold_up(g - 1, masked[(g - 1) % 2])
+        if g < 8:
+            masked[g % 2] = kept(prods[g % 2])
 
     pl.semaphore_wait(barrier, jnp.where(core == xh, 31, 32))
 
@@ -271,6 +291,7 @@
 
 
 def body(facet_positions, reflectivity, block_building, visible, platform):
+    args = (facet_positions, reflectivity, block_building, visible.T, platform)
     anywhere = pl.BlockSpec(memory_space=pltpu.HBM)
     return pl.pallas_call(
         kernel,
@@ -298,14 +319,16 @@
             pltpu.VMEM((2, 256, 128), F32),
             pltpu.VMEM((256, 256), BF16),
             pltpu.VMEM((2, 16, 128), F32),
+            pltpu.VMEM((2, 256, 256), F32),
+            pltpu.VMEM((2, 128, 512), BF16),
             pltpu.SemaphoreType.DMA((5,)),
             pltpu.SemaphoreType.DMA((3,)),
             pltpu.SemaphoreType.DMA((3,)),
         ],
         compiler_params=pltpu.CompilerParams(
-            collective_id=0, has_side_effects=True, vmem_limit_bytes=62 * 1024 * 1024
+            collective_id=0, has_side_effects=True, vmem_limit_bytes=48 * 1024 * 1024
         ),
-    )(facet_positions, reflectivity, block_building, visible.T, platform)
+    )(*[pltpu.with_memory_space_constraint(x, pltpu.HBM) for x in args])
 
 
 def solution(mesh):

time: 33.5 us -> 31.6 us (0.943)
  Pallas kernels: 32 us -> 30.9 us
  local copies, waits for them, and re-layouts: 1.32 us -> 0.61 us
    pallas_call x1, Pallas kernels: 32 us -> 30.9 us  [body(): pl.pallas_call(kernel, out_shape=jax.ShapeDtypeStruct((2, 16, 128), F32),...]
    unnamed x1, local copies, waits for them, and re-layouts: 1.32 us -> 0.61 us
where the time goes in v3:
time: 31.6 us; the launch traced here: 31.5 us
  Pallas kernels  30.9 us (98%)
  local copies, waits for them, and re-layouts  0.61 us (2%)
    pallas_call x1, Pallas kernels, body(): pl.pallas_call(kernel, out_shape=jax.ShapeDtypeStruct((2, 16, 128), F32),...  30.9 us

profile of v3, /device:TPU:1, one launch (start us, length us, event | category | flops | bytes accessed | tf_op | source)
XLA Modules:
  0.0 31.5 jit_solution(3389663891009003358)
XLA Ops:
  0.0 30.9 %shard_map.55 = f32[2,16,128]{2,1,0:T(8,128)S(1)} custom-call(f32[3,768]{1,0:T(4,128)} %fp_hbm.1, f32[2,768]{1,0:T(2,128)} %rf_hbm.1, s32[6]{0:T(128)} %bb_hbm.1, s32[2,24]{1,0:T(2,128)} %bitcast.1, f32[3,64]{1,0:T(4,128)} %plat_hbm.1), custom_call_target="tpu_custom_call" | custom-call | tf_op jit(solution)/shard_map/pallas_call | solution.py:296
  30.9 0.6 %copy.7 = f32[2,16,128]{2,1,0:T(8,128)} copy(f32[2,16,128]{2,1,0:T(8,128)S(1)} %shard_map.55) | data formatting | bytes 32768
